TPU v7x, 32 devices: a whole 2x2x4 slice. The times are simulated.
32 devices in a mesh: gx: 4 (over y, x), gz: 2 (over core), ta: 4 (over z).
Axes of the slice: x: 2, y: 2, z: 4, core: 2. Of those that a mesh axis runs over, the one named last changes fastest.
Arguments:
- right_side: float32 [512, 64, 128], P(('gx', 'ta'), 'gz'), may hold values from -8 to 8
- diagonal: float32 [512, 64, 128], P(('gx', 'ta'), 'gz'), may hold values from 0.05 to 1
- coupling: float32 [128, 128], replicated, as said below
- wall_owner: int32 [2048, 1], P(('gx', 'gz', 'ta')), may hold values from 0 to 15; in each aligned block of 64 rows (0 to 63, 64 to 127, ...) at most 8 rows name the same one
- neighbours: int32 [2048, 4], P(('gx', 'gz', 'ta')), may hold values from 0 to 63
- input_weight: bfloat16 [256, 128], replicated, may hold values from -0.375 to 0.375
- head_weights: bfloat16 [16, 128, 128], P(('gx', 'ta')), may hold values from -0.5 to 0.5
- output_weight: float32 [128], replicated, may hold values from -0.5 to 0.5
Outputs:
- solution_field: float32 [512, 64, 128], P(('gx', 'ta'), 'gz')
- residual: float32 [512, 64, 128], P(('gx', 'ta'), 'gz')
- input_grad: float32 [256, 128], replicated
- head_grad: float32 [16, 128, 128], P(('gx', 'ta'))
- output_grad: float32 [128], replicated
Inputs may be any that keep to these rules, and one draw needn't show every extreme that they name: `wall_owner`: among the wall elements of one device, no trainer is named more than 8 times, a bound that some block reaches. `neighbours`: each entry is a local element number of the element's own device. `coupling`: Symmetric; diagonal entries between 0.4 and 1.4; off-diagonal entries of magnitude at most 0.25 / sqrt(128).
All inputs are finite; a program needn't handle non-finite values.
Results may differ from a plain program's by a relative error of at most 0.004.
Values may be sent and summed in bfloat16 or wider, within the bound.
A program may use at most 64 MiB of HBM per device.

v0:
```python
import jax
import jax.numpy as jnp
from jax import lax
from jax.sharding import PartitionSpec as P

EL = 4
ITERS = 6


def padded_2(block, sides, width):
    for axis, dim in sides:
        count = lax.axis_size(axis)
        forward = [(i, i + 1) for i in range(count - 1)]
        forward.append((count - 1, 0))
        backward = [(target, source) for source, target in forward]
        low = lax.ppermute(
            lax.slice_in_dim(block, block.shape[dim] - width, None, axis=dim), axis, forward
        )
        high = lax.ppermute(lax.slice_in_dim(block, 0, width, axis=dim), axis, backward)
        block = jnp.concatenate([low, block, high], axis=dim)
    return block


def silu_slope(inputs):
    sigmoid_val = jax.nn.sigmoid(inputs)
    return sigmoid_val * (1.0 + inputs * (1.0 - sigmoid_val))


def apply_op(grid_field, diagonal, coupling):
    padded = padded_2(grid_field, ((("gx", "ta"), 0), ("gz", 1)), 1)
    beside = padded[2:, 1:-1] + padded[:-2, 1:-1] + padded[1:-1, 2:] + padded[1:-1, :-2]
    depth = grid_field.shape[2]
    normal_part = jnp.dot(
        grid_field.reshape(-1, depth), coupling, precision=lax.Precision.HIGHEST
    ).reshape(grid_field.shape)
    return (4.0 + diagonal) * grid_field - beside + normal_part


def global_squares(residual):
    return lax.psum(jnp.sum(residual * residual), ("gx", "gz", "ta"))


def pool(grid_vals):
    trailing = grid_vals.shape[2:]
    rows_here = grid_vals.shape[0]
    cols_here = grid_vals.shape[1]
    shaped = grid_vals.reshape((rows_here // EL, EL, cols_here // EL, EL) + trailing)
    return jnp.sum(shaped, axis=(1, 3)) / EL


def owner_step(hidden, shear, own_head, output_weight, elements):
    head_pre = jnp.dot(hidden, own_head, preferred_element_type=jnp.float32)
    head_out = jax.nn.silu(head_pre)
    predicted = jnp.sum(head_out * output_weight, axis=1)
    misfit = (predicted - shear.astype(jnp.float32)) / elements
    output_part = jnp.sum(misfit[:, None] * head_out, axis=0)
    head_back = (misfit[:, None] * output_weight * silu_slope(head_pre)).astype(jnp.bfloat16)
    head_part = jnp.einsum("rk,rl->kl", hidden, head_back, preferred_element_type=jnp.float32)
    hidden_back = jnp.einsum(
        "rl,kl->rk", head_back, own_head, preferred_element_type=jnp.float32
    ).astype(jnp.bfloat16)
    return (head_part, output_part, hidden_back)


def local(
    right_side,
    diagonal,
    coupling,
    wall_owner,
    neighbours,
    input_weight,
    head_weights,
    output_weight,
):
    solution_field = jnp.zeros_like(right_side)
    residual = right_side

    def plain_iter(index, state):
        solution_now, residual_now, direction, norm_now = state
        applied = apply_op(direction, diagonal, coupling)
        curv_sum = lax.psum(jnp.sum(direction * applied), ("gx", "gz", "ta"))
        step_size = norm_now / curv_sum
        solution_now = solution_now + step_size * direction
        residual_now = residual_now - step_size * applied
        norm_next = global_squares(residual_now)
        direction = residual_now + norm_next / norm_now * direction
        return (solution_now, residual_now, direction, norm_next)

    start_norm = global_squares(residual)
    solution_field, residual, unused_dir, unused_norm = lax.fori_loop(
        0, ITERS, plain_iter, (solution_field, residual, right_side, start_norm)
    )
    depth = solution_field.shape[2]
    wall_feat = pool(solution_field).reshape(-1, depth).astype(jnp.bfloat16)
    wall_shear = (
        pool(solution_field[:, :, 1] - solution_field[:, :, 0]).reshape(-1).astype(jnp.bfloat16)
    )
    graph_mean = jnp.mean(wall_feat.astype(jnp.float32)[neighbours], axis=1).astype(jnp.bfloat16)
    node_input = jnp.concatenate([wall_feat, graph_mean], axis=1)
    elements = node_input.shape[0]
    trainers = lax.axis_size(("gx", "ta"))
    capacity = max(2, 2 * elements // trainers)
    owners = wall_owner[:, 0]
    owner_hits = (owners[:, None] == jnp.arange(trainers, dtype=jnp.int32)[None, :]).astype(
        jnp.int32
    )
    slot_index = jnp.sum(jnp.cumsum(owner_hits, axis=0) * owner_hits, axis=1) - 1

    def pack(values):
        holder = jnp.zeros((trainers, capacity) + values.shape[1:], values.dtype)
        return holder.at[owners, slot_index].set(values)

    packed_shear = pack(wall_shear)
    own_head = head_weights[0]
    preact = jnp.dot(node_input, input_weight, preferred_element_type=jnp.float32)
    hidden = jax.nn.silu(preact).astype(jnp.bfloat16)
    arrived, arrived_shear = (
        lax.all_to_all(pack(hidden), ("gx", "ta"), split_axis=0, concat_axis=0, tiled=True),
        lax.all_to_all(packed_shear, ("gx", "ta"), split_axis=0, concat_axis=0, tiled=True),
    )
    head_part, output_part, hidden_back = owner_step(
        arrived.reshape(-1, arrived.shape[2]),
        arrived_shear.reshape(-1),
        own_head,
        output_weight,
        elements,
    )
    returned = lax.all_to_all(
        hidden_back.reshape(trainers, capacity, -1),
        ("gx", "ta"),
        split_axis=0,
        concat_axis=0,
        tiled=True,
    )
    preact_back = (returned[owners, slot_index].astype(jnp.float32) * silu_slope(preact)).astype(
        jnp.bfloat16
    )
    input_part = jnp.einsum(
        "rk,rl->kl", node_input, preact_back, preferred_element_type=jnp.float32
    )
    head_total = lax.psum(head_part, "gz")
    input_total, output_total = lax.psum((input_part, output_part), ("gx", "gz", "ta"))
    return (solution_field, residual, input_total, head_total[None], output_total)


def solution(mesh):
    placed = (
        P(("gx", "ta"), "gz", None),
        P(("gx", "ta"), "gz", None),
        P(),
        P(("gx", "gz", "ta"), None),
        P(("gx", "gz", "ta"), None),
        P(),
        P(("gx", "ta"), None, None),
        P(),
    )
    return jax.shard_map(
        local,
        mesh=mesh,
        in_specs=placed,
        out_specs=(
            P(("gx", "ta"), "gz", None),
            P(("gx", "ta"), "gz", None),
            P(),
            P(("gx", "ta"), None, None),
            P(),
        ),
        check_vma=False,
    )
```

profile of v0, /device:TPU:0, one launch (start us, length us, event | category | flops | bytes accessed | tf_op | source)
XLA Modules:
  0.0 830.1 jit_solution(5512780398262250563)
XLA Ops:
  9.0 42.2 %psum.42 = f32[]{:T(128)} all-reduce(f32[]{:T(128)} %multiply_reduce_fusion.2), channel_id=1, replica_groups=mesh['gx'=4,'gz'=2,'ta'=4] {'gx','gz','ta'}, use_global_device_ids=true, to_apply=%region_1.0 | all-reduce | flops 1 | bytes 8 | tf_op jit(solution)/shard_map/psum | solution.py:40
  52.7 575.8 %while.17 = (s32[]{:T(128)}, f32[32,32,128]{2,1,0:T(8,128)S(1)}, f32[32,32,128]{2,1,0:T(8,128)S(1)}, f32[32,32,128]{2,1,0:T(8,128)S(1)}, f32[]{:T(128)}, /*index...) while((s32[]{:T(128)}, f32[32,32,128]{2,1,0:T(8,128)S(1)}, ...), condition=%wide.region_7.0_spmd.clone, body=%wide.region_2.0_spmd.clone.sunk | while | flops 204210176 | bytes 7977291 | solution.py:90
  54.2 4.1 collective-permute-start.1
  58.4 1.7 collective-permute-done
  62.9 41.0 %psum.50 = f32[]{:T(128)} all-reduce(f32[]{:T(128)} %get-tuple-element.161), channel_id=1, replica_groups=mesh['gx'=4,'gz'=2,'ta'=4] {'gx','gz','ta'}, use_global_device_ids=true, to_apply=%region_4.0 | all-reduce | flops 1 | bytes 8 | tf_op jit(solution)/shard_map/while/body/eval_jaxpr/psum | solution.py:81
  105.5 42.1 %psum.51 = f32[]{:T(128)} all-reduce(f32[]{:T(128)} %get-tuple-element.163), channel_id=1, replica_groups=mesh['gx'=4,'gz'=2,'ta'=4] {'gx','gz','ta'}, use_global_device_ids=true, to_apply=%region_6.0 | all-reduce | flops 1 | bytes 8 | tf_op jit(solution)/shard_map/while/body/eval_jaxpr/psum | solution.py:40
  148.7 5.6 collective-permute-start.1
  154.3 1.7 collective-permute-done
  158.9 41.0 %psum.50 = f32[]{:T(128)} all-reduce(f32[]{:T(128)} %get-tuple-element.161), channel_id=1, replica_groups=mesh['gx'=4,'gz'=2,'ta'=4] {'gx','gz','ta'}, use_global_device_ids=true, to_apply=%region_4.0 | all-reduce | flops 1 | bytes 8 | tf_op jit(solution)/shard_map/while/body/eval_jaxpr/psum | solution.py:81
  201.5 42.1 %psum.51 = f32[]{:T(128)} all-reduce(f32[]{:T(128)} %get-tuple-element.163), channel_id=1, replica_groups=mesh['gx'=4,'gz'=2,'ta'=4] {'gx','gz','ta'}, use_global_device_ids=true, to_apply=%region_6.0 | all-reduce | flops 1 | bytes 8 | tf_op jit(solution)/shard_map/while/body/eval_jaxpr/psum | solution.py:40
  244.7 5.6 collective-permute-start.1
  254.9 41.0 %psum.50 = f32[]{:T(128)} all-reduce(f32[]{:T(128)} %get-tuple-element.161), channel_id=1, replica_groups=mesh['gx'=4,'gz'=2,'ta'=4] {'gx','gz','ta'}, use_global_device_ids=true, to_apply=%region_4.0 | all-reduce | flops 1 | bytes 8 | tf_op jit(solution)/shard_map/while/body/eval_jaxpr/psum | solution.py:81
  297.5 42.1 %psum.51 = f32[]{:T(128)} all-reduce(f32[]{:T(128)} %get-tuple-element.163), channel_id=1, replica_groups=mesh['gx'=4,'gz'=2,'ta'=4] {'gx','gz','ta'}, use_global_device_ids=true, to_apply=%region_6.0 | all-reduce | flops 1 | bytes 8 | tf_op jit(solution)/shard_map/while/body/eval_jaxpr/psum | solution.py:40
  340.7 5.6 collective-permute-start.1
  346.3 1.7 collective-permute-done
  350.9 41.0 %psum.50 = f32[]{:T(128)} all-reduce(f32[]{:T(128)} %get-tuple-element.161), channel_id=1, replica_groups=mesh['gx'=4,'gz'=2,'ta'=4] {'gx','gz','ta'}, use_global_device_ids=true, to_apply=%region_4.0 | all-reduce | flops 1 | bytes 8 | tf_op jit(solution)/shard_map/while/body/eval_jaxpr/psum | solution.py:81
  393.5 42.1 %psum.51 = f32[]{:T(128)} all-reduce(f32[]{:T(128)} %get-tuple-element.163), channel_id=1, replica_groups=mesh['gx'=4,'gz'=2,'ta'=4] {'gx','gz','ta'}, use_global_device_ids=true, to_apply=%region_6.0 | all-reduce | flops 1 | bytes 8 | tf_op jit(solution)/shard_map/while/body/eval_jaxpr/psum | solution.py:40
  436.7 5.6 collective-permute-start.1
  446.8 41.0 %psum.50 = f32[]{:T(128)} all-reduce(f32[]{:T(128)} %get-tuple-element.161), channel_id=1, replica_groups=mesh['gx'=4,'gz'=2,'ta'=4] {'gx','gz','ta'}, use_global_device_ids=true, to_apply=%region_4.0 | all-reduce | flops 1 | bytes 8 | tf_op jit(solution)/shard_map/while/body/eval_jaxpr/psum | solution.py:81
  489.4 42.1 %psum.51 = f32[]{:T(128)} all-reduce(f32[]{:T(128)} %get-tuple-element.163), channel_id=1, replica_groups=mesh['gx'=4,'gz'=2,'ta'=4] {'gx','gz','ta'}, use_global_device_ids=true, to_apply=%region_6.0 | all-reduce | flops 1 | bytes 8 | tf_op jit(solution)/shard_map/while/body/eval_jaxpr/psum | solution.py:40
  532.7 5.6 collective-permute-start.1
  542.8 41.0 %psum.50 = f32[]{:T(128)} all-reduce(f32[]{:T(128)} %get-tuple-element.161), channel_id=1, replica_groups=mesh['gx'=4,'gz'=2,'ta'=4] {'gx','gz','ta'}, use_global_device_ids=true, to_apply=%region_4.0 | all-reduce | flops 1 | bytes 8 | tf_op jit(solution)/shard_map/while/body/eval_jaxpr/psum | solution.py:81
  585.4 42.1 %psum.51 = f32[]{:T(128)} all-reduce(f32[]{:T(128)} %get-tuple-element.163), channel_id=1, replica_groups=mesh['gx'=4,'gz'=2,'ta'=4] {'gx','gz','ta'}, use_global_device_ids=true, to_apply=%region_6.0 | all-reduce | flops 1 | bytes 8 | tf_op jit(solution)/shard_map/while/body/eval_jaxpr/psum | solution.py:40
  629.6 3.6 scatter_fusion.1
  633.9 5.6 all-to-all-start.1
  642.2 7.3 scatter_fusion
  649.5 7.1 all-to-all-start
  656.7 7.2 all-to-all-done
  665.1 3.5 all-to-all-start.2
  669.6 6.4 all-to-all-done.2
  677.6 38.5 %psum.45 = f32[128]{0:T(128)} all-reduce(f32[128]{0:T(128)S(1)} %get-tuple-element.97), channel_id=1, replica_groups=mesh['gx'=4,'gz'=2,'ta'=4] {'gx','gz','ta'}, use_global_device_ids=true, to_apply=%region_19.20 | all-reduce | flops 128 | bytes 1024 | tf_op jit(solution)/shard_map/psum | solution.py:142
  716.1 105.0 %all-reduce.3.cloned.1.call-done = f32[256,128]{1,0:T(8,128)} async-done(((f32[256,128]{1,0:T(8,128)}), f32[256,128]{1,0:T(8,128)}) %all-reduce.3.cloned.1.call-update) | async-done | bytes 131088 | tf_op jit(solution)/shard_map/psum | solution.py:142
  (150 shorter events, 41.0 us)
Async XLA Ops:
  7.2 634.2 %copy-start = (bf16[256,128]{1,0:T(8,128)(2,1)S(1)}, bf16[256,128]{1,0:T(8,128)(2,1)}, u32[]{:S(2)}) copy-start(bf16[256,128]{1,0:T(8,128)(2,1)} %param.15) | copy-start | bytes 196612
  8.3 44.0 %copy-start.8 = (f32[32,32,128]{2,1,0:T(8,128)S(1)}, f32[32,32,128]{2,1,0:T(8,128)}, u32[]{:S(2)}) copy-start(f32[32,32,128]{2,1,0:T(8,128)} %param.11) | copy-start | bytes 1572868
  52.7 7.3 collective-permute-start
  54.2 5.9 collective-permute-start.1
  60.2 1.3 collective-permute-start.2
  60.3 1.3 collective-permute-start.3
  148.7 7.4 collective-permute-start
  148.7 7.4 collective-permute-start.1
  156.2 1.3 collective-permute-start.2
  156.2 1.3 collective-permute-start.3
  244.6 7.4 collective-permute-start
  244.7 7.4 collective-permute-start.1
  252.1 1.3 collective-permute-start.2
  252.2 1.3 collective-permute-start.3
  340.6 7.4 collective-permute-start
  340.7 7.4 collective-permute-start.1
  348.1 1.3 collective-permute-start.2
  348.2 1.3 collective-permute-start.3
  436.6 7.4 collective-permute-start
  436.7 7.4 collective-permute-start.1
  444.1 1.3 collective-permute-start.2
  444.2 1.3 collective-permute-start.3
  532.6 7.4 collective-permute-start
  532.7 7.4 collective-permute-start.1
  540.1 1.3 collective-permute-start.2
  540.2 1.3 collective-permute-start.3
  633.9 15.6 %all-to-all-start.1 = ((bf16[16,1,8]{2,1,0:T(2,128)(2,1)}), bf16[16,1,8]{2,1,0:T(2,128)(2,1)S(1)}, u32[]{:S(2)}, u32[]{:S(2)}) async-start(bf16[16,1,8]{2,1,0:T(2,128)(2,1)} %copy.17), calls=%async_computation.1 | async-start | bytes 16384 | tf_op jit(solution)/shard_map/all_to_all | solution.py:119
  649.5 14.5 %copy-start.4 = (bf16[1,128,128]{2,1,0:T(8,128)(2,1)S(1)}, bf16[1,128,128]{2,1,0:T(8,128)(2,1)}, u32[]{:S(2)}) copy-start(bf16[1,128,128]{2,1,0:T(8,128)(2,1)} %param.16) | copy-start | bytes 98308
  649.5 14.5 %all-to-all-start = ((bf16[16,8,128]{2,1,0:T(8,128)(2,1)}), bf16[16,8,128]{2,1,0:T(8,128)(2,1)S(1)}, u32[]{:S(2)}, u32[]{:S(2)}) async-start(bf16[16,8,128]{2,1,0:T(8,128)(2,1)} %scatter_fusion), calls=%async_computation | async-start | bytes 65536 | tf_op jit(solution)/shard_map/all_to_all | solution.py:118
  665.1 10.8 %all-to-all-start.2 = ((bf16[16,8,128]{2,1,0:T(8,128)(2,1)}), bf16[16,8,128]{2,1,0:T(8,128)(2,1)S(1)}, u32[]{:S(2)}, u32[]{:S(2)}) async-start(bf16[16,8,128]{2,1,0:T(8,128)(2,1)} %fusion.9), calls=%async_computation.2 | async-start | bytes 65536 | tf_op jit(solution)/shard_map/all_to_all | solution.py:128
  668.6 47.5 %all-reduce.5.cloned.1.call-start = ((), (), s32[]{:S(2)}) async-start(), calls=%async_computation.4 | async-start | bytes 131072 | tf_op jit(solution)/shard_map/psum | solution.py:141
  669.5 151.6 %all-reduce.3.cloned.1.call-start = ((), (), s32[]{:S(2)}) async-start(), calls=%async_computation.3 | async-start | bytes 262144 | tf_op jit(solution)/shard_map/psum | solution.py:142
  (7 other events, 22.8 us)
Sparse Core Ops, SparseCore 0:
  672.3 18.9 all-reduce.4
  697.4 123.5 all-reduce.2
where the time goes:
time: 834 us; the launch traced here: 830 us
  blocking collectives  579 us (69%)
  waiting for transfers between devices  130 us (16%)
  starting transfers between devices  53.6 us (6%)
  local copies, waits for them, and re-layouts  20.2 us (2%)
  between operations  14.3 us (2%)
  loops' own time  12.5 us (1%)
  matrix products  10.8 us (1%)
  other arithmetic  9.36 us (1%)
    psum x7, blocking collectives, global_squares(): return lax.psum(jnp.sum(residual * residual), ('gx', 'gz', 'ta'))  295 us
    psum x6, blocking collectives, plain_iter(): curv_sum = lax.psum(jnp.sum(direction * applied), ('gx', 'gz', 'ta'))  246 us
    psum x1, waiting for transfers between devices, local(): lax.psum((input_part, output_part), ('gx', 'gz', 'ta'))  105 us
    psum x1, blocking collectives, local(): lax.psum((input_part, output_part), ('gx', 'gz', 'ta'))  38.5 us
    ppermute x12, starting transfers between devices, padded_2(): lax.ppermute(lax.slice_in_dim(block, 0, width, axis=dim), axis, backward)  35.1 us
  transfers between devices with their start and end apart: 29, of which 15 were waited for; matrix products, arithmetic and copies ran while one was open for 1% of the time, Pallas kernels for 0%

commit v1 on v0

v1 whole, which is shorter than its diff:
```python
import functools
import jax
import jax.numpy as jnp
from jax import lax
from jax.experimental import pallas as pl
from jax.experimental.pallas import tpu as pltpu
from jax.sharding import PartitionSpec as P

EL = 4
ITERS = 6
HX = ITERS
HZ = 8
CENTRE = 5.3
SPREAD = 5.4
PLANES = 14
MESH = pl.DeviceIdType.MESH
F32 = jnp.float32
BF16 = jnp.bfloat16

DIRS = [(dx, dz) for dx in (-1, 0, 1) for dz in (-1, 0, 1) if (dx, dz) != (0, 0)]


def tree_sum(terms):
    terms = list(terms)
    while len(terms) > 1:
        terms = [
            terms[i] + terms[i + 1] if i + 1 < len(terms) else terms[i]
            for i in range(0, len(terms), 2)
        ]
    return terms[0]


def sigmoid(v):
    return 1.0 / (1.0 + jnp.exp(-v))


def dot_rows(a, b):
    return lax.dot_general(a, b, (((0,), (0,)), ((), ())), preferred_element_type=F32)


def dot_lanes(a, b):
    return lax.dot_general(a, b, (((1,), (1,)), ((), ())), preferred_element_type=F32)


def kernel(
    sizes,
    rhs_hbm,
    diag_hbm,
    coup_ref,
    owner_ref,
    neigh_ref,
    w_in_ref,
    head_ref,
    w_out_ref,
    x_ref,
    r_ref,
    ig_ref,
    hg_ref,
    og_ref,
    basis,
    diag,
    heads,
    c_split,
    gram_send,
    gram_buf,
    pooled,
    packed,
    part,
    msg_send,
    msg_buf,
    fin,
    load_sem,
    halo_send,
    halo_recv,
    heads_send,
    heads_recv,
    gram_ssem,
    gram_rsem,
    msg_ssem,
    msg_rsem,
    fin_ssem,
    fin_rsem,
):
    n_gx, n_gz, n_ta = sizes
    count = n_gx * n_gz * n_ta
    trainers = n_gx * n_ta
    cx, cz, depth = x_ref.shape
    ex, ez = cx + 2 * HX, cz + 2 * HZ
    elements = owner_ref.shape[0]
    half = packed.shape[1] // 2
    chunks = fin.shape[0]
    gx, gz, ta = lax.axis_index("gx"), lax.axis_index("gz"), lax.axis_index("ta")
    me = (gx * n_gz + gz) * n_ta + ta
    row = gx * n_ta + ta

    def coords(d):
        return (d // (n_gz * n_ta), (d // n_ta) % n_gz, d % n_ta)

    load_rhs = pltpu.make_async_copy(
        rhs_hbm, basis.at[1, pl.ds(HX, cx), pl.ds(HZ, cz), :], load_sem.at[0]
    )
    load_diag = pltpu.make_async_copy(
        diag_hbm, diag.at[pl.ds(HX, cx), pl.ds(HZ, cz), :], load_sem.at[1]
    )
    load_rhs.start()
    load_diag.start()

    barrier = pltpu.get_barrier_semaphore()

    def greet(s, carry):
        pl.semaphore_signal(
            barrier, inc=1, device_id=coords((me + s) % count), device_id_type=MESH
        )
        return carry

    lax.fori_loop(1, count, greet, 0)

    basis[0] = jnp.zeros(basis.shape[1:], F32)
    scaled = coup_ref[...] * (2.0 / SPREAD)
    c_hi = scaled.astype(BF16)
    c_lo = (scaled - c_hi.astype(F32)).astype(BF16)
    c_split[0:depth, 0:depth] = c_hi
    c_split[0:depth, depth : 2 * depth] = c_lo
    c_split[depth : 2 * depth, 0:depth] = c_hi
    c_split[depth : 2 * depth, depth : 2 * depth] = c_lo
    heads[row] = head_ref[0]

    load_rhs.wait()
    load_diag.wait()
    pl.semaphore_wait(barrier, count - 1)

    def span(step, ghost, inner):
        if step == 0:
            return (ghost, inner), (ghost, inner)
        if step == 1:
            return (inner, ghost), (0, ghost)
        return (ghost, ghost), (ghost + inner, ghost)

    halos = []
    for i, (dx, dz) in enumerate(DIRS):
        (sx, nx), (tx, unused_nx) = span(dx, HX, cx)
        (sz, nz), (tz, unused_nz) = span(dz, HZ, cz)
        there = (row + dx + trainers) % trainers
        target = (there // n_ta, (gz + dz + n_gz) % n_gz, there % n_ta)
        for j, ref in enumerate((basis.at[1], diag)):
            halos.append(
                pltpu.make_async_remote_copy(
                    src_ref=ref.at[pl.ds(sx, nx), pl.ds(sz, nz), :],
                    dst_ref=ref.at[pl.ds(tx, nx), pl.ds(tz, nz), :],
                    send_sem=halo_send.at[j, i],
                    recv_sem=halo_recv.at[j, i],
                    device_id=target,
                    device_id_type=MESH,
                )
            )
    for copy in halos:
        copy.start()

    def send_heads(s, carry):
        there = (row + s) % trainers
        pltpu.make_async_remote_copy(
            src_ref=heads.at[row],
            dst_ref=heads.at[row],
            send_sem=heads_send,
            recv_sem=heads_recv,
            device_id=(there // n_ta, gz, there % n_ta),
            device_id_type=MESH,
        ).start()
        return carry

    lax.fori_loop(1, trainers, send_heads, 0)
    for copy in halos:
        copy.wait()

    rows = PLANES * ez

    def grow(k, carry):
        def planes(j, inner_carry):
            x0 = 1 + PLANES * j
            cur = basis[k + 1, pl.ds(x0, PLANES)].reshape(rows, depth)
            up = basis[k + 1, pl.ds(x0 - 1, PLANES)].reshape(rows, depth)
            down = basis[k + 1, pl.ds(x0 + 1, PLANES)].reshape(rows, depth)
            prev = basis[k, pl.ds(x0, PLANES)].reshape(rows, depth)
            own = diag[pl.ds(x0, PLANES)].reshape(rows, depth)
            hi = cur.astype(BF16)
            lo = (cur - hi.astype(F32)).astype(BF16)
            prod = jnp.dot(
                jnp.concatenate([hi, lo], axis=1), c_split[...], preferred_element_type=F32
            )
            beside = (up + down) + (pltpu.roll(cur, 1, 0) + pltpu.roll(cur, rows - 1, 0))
            horizontal = ((own + (4.0 - CENTRE)) * cur - beside) * (2.0 / SPREAD)
            new = horizontal + (prod[:, 0:depth] + prod[:, depth : 2 * depth]) - prev
            basis[k + 2, pl.ds(x0, PLANES)] = new.reshape(PLANES, ez, depth)
            return inner_carry

        return lax.fori_loop(0, (ex - 2) // PLANES, planes, carry)

    lax.fori_loop(0, ITERS, grow, 0)

    pairs = [(i, j) for i in range(ITERS + 1) for j in range(i, ITERS + 1)]
    spot = {pair: k for k, pair in enumerate(pairs)}

    def gram_plane(x, sums):
        sums = list(sums)
        for z in range(0, cz, 8):
            vecs = [basis[k + 1, HX + x, HZ + z : HZ + z + 8, :] for k in range(ITERS + 1)]
            for q, (i, j) in enumerate(pairs):
                sums[q] = sums[q] + vecs[i] * vecs[j]
        return tuple(sums)

    sums = lax.fori_loop(
        0, cx, gram_plane, tuple(jnp.zeros((8, depth), F32) for unused in pairs)
    )
    lane = lax.broadcasted_iota(jnp.int32, (8, depth), 1)
    mine = jnp.zeros((8, depth), F32)
    for q, value in enumerate(sums):
        mine = mine + jnp.where(lane == q, jnp.sum(value, axis=1, keepdims=True), 0.0)
    mine = jnp.sum(mine, axis=0, keepdims=True)
    gram_send[...] = mine
    gram_buf[me] = mine

    def send_gram(s, carry):
        pltpu.make_async_remote_copy(
            src_ref=gram_send,
            dst_ref=gram_buf.at[me],
            send_sem=gram_ssem,
            recv_sem=gram_rsem,
            device_id=coords((me + s) % count),
            device_id_type=MESH,
        ).start()
        return carry

    lax.fori_loop(1, count, send_gram, 0)

    def all_bytes(ref, number, sem):
        there = ref.at[pl.ds(0, number)]
        return pltpu.make_async_copy(there, there, sem)

    owner = owner_ref[...]
    trainer_ids = lax.broadcasted_iota(jnp.int32, (elements, 128), 1)
    hits = jnp.where(owner == trainer_ids, 1.0, 0.0).astype(BF16)
    same = dot_lanes(hits, hits)
    e_row = lax.broadcasted_iota(jnp.int32, (elements, elements), 0)
    e_col = lax.broadcasted_iota(jnp.int32, (elements, elements), 1)
    rank = jnp.sum(jnp.where(e_col < e_row, same, 0.0), axis=1, keepdims=True)
    slot = owner.astype(F32) * (2.0 * half) + rank
    slot_ids = lax.broadcasted_iota(jnp.int32, (elements, trainers * 2 * half), 1).astype(F32)
    place_hidden = jnp.where(slot == slot_ids, 1.0, 0.0).astype(BF16)
    place_back = jnp.where(slot + half == slot_ids, 1.0, 0.0).astype(BF16)
    place = jnp.concatenate([place_hidden, place_back], axis=0)
    neigh = neigh_ref[...]
    links = jnp.zeros((elements, elements), F32)
    for j in range(neigh.shape[1]):
        links = links + jnp.where(neigh[:, j : j + 1] == e_col, 1.0, 0.0)
    links = links.astype(BF16)
    pool_cols = lax.broadcasted_iota(jnp.int32, (elements, elements * EL), 1)
    pool_rows = lax.broadcasted_iota(jnp.int32, (elements, elements * EL), 0) * EL
    pool_map = jnp.where(
        (pool_cols >= pool_rows) & (pool_cols < pool_rows + EL), 1.0, 0.0
    ).astype(F32)

    all_bytes(gram_buf, count - 1, gram_rsem).wait()
    total = jnp.sum(gram_buf[...], axis=0)

    gram = {}
    for (i, j), q in spot.items():
        value = jnp.broadcast_to(total[0:1, q : q + 1], (8, depth))
        gram[i, j] = value
        gram[j, i] = value

    def inner(a, b):
        return tree_sum(
            a[i] * tree_sum(gram[i, j] * b[j] for j in range(len(b))) for i in range(len(a))
        )

    def operate(a):
        out = []
        for i in range(len(a) + 1):
            terms = []
            if i < len(a):
                terms.append(CENTRE * a[i])
            if i >= 1:
                terms.append((SPREAD / 2) * a[i - 1])
            if i + 1 < len(a):
                terms.append((SPREAD / 2) * a[i + 1])
            out.append(tree_sum(terms))
        return out

    one = jnp.ones((8, depth), F32)
    res, way, sol = [one], [one], []
    norm_now = gram[0, 0]
    for it in range(ITERS):
        applied = operate(way)
        step = norm_now / inner(way, applied)
        sol = [
            sol[i] + step * way[i] if i < len(sol) else step * way[i] for i in range(len(way))
        ]
        res = [
            res[i] - step * applied[i] if i < len(res) else -(step * applied[i])
            for i in range(len(applied))
        ]
        if it < ITERS - 1:
            norm_next = inner(res, res)
            ratio = norm_next / norm_now
            way = [res[i] + ratio * way[i] if i < len(way) else res[i] for i in range(len(res))]
            norm_now = norm_next

    def combine(coefs, x0):
        return tree_sum(
            coefs[k][None]
            * basis[k + 1, pl.ds(HX + x0, EL), HZ : HZ + cz, :].reshape(EL * cz // 8, 8, depth)
            for k in range(len(coefs))
        ).reshape(EL, cz, depth)

    def solve_planes(g, carry):
        field = combine(sol, g * EL)
        x_ref[pl.ds(g * EL, EL)] = field
        pooled[pl.ds(pl.multiple_of(g * cz, cz), cz), :] = jnp.sum(field, axis=0)
        return carry

    lax.fori_loop(0, cx // EL, solve_planes, 0)

    feat = (
        jnp.dot(
            pool_map, pooled[...], precision=lax.Precision.HIGHEST, preferred_element_type=F32
        )
        * (1.0 / EL)
    )
    shear = (feat[:, 1:2] - feat[:, 0:1]).astype(BF16).astype(F32)
    wall_feat = feat.astype(BF16)
    graph_mean = (jnp.dot(links, wall_feat, preferred_element_type=F32) * 0.25).astype(BF16)
    node_input = jnp.concatenate([wall_feat, graph_mean], axis=1)
    preact = jnp.dot(node_input, w_in_ref[...], preferred_element_type=F32)
    pre_sig = sigmoid(preact)
    hidden = (preact * pre_sig).astype(BF16)
    all_bytes(heads, trainers - 1, heads_recv).wait()

    def forward(t, acc):
        value = jnp.dot(hidden, heads[t], preferred_element_type=F32)
        return jnp.where(owner == t, value, acc)

    group = 16
    def forward_group(g, acc):
        for t in range(group):
            acc = forward(g * group + t, acc)
        return acc

    head_pre = lax.fori_loop(
        0, trainers // group, forward_group, jnp.zeros((elements, depth), F32)
    )
    head_sig = sigmoid(head_pre)
    head_out = head_pre * head_sig
    w_out = w_out_ref[...]
    predicted = jnp.sum(head_out * w_out, axis=1, keepdims=True)
    misfit = (predicted - shear) * (1.0 / elements)
    out_part = jnp.sum(misfit * head_out, axis=0, keepdims=True)
    head_back_f = misfit * w_out * (head_sig * (1.0 + head_pre * (1.0 - head_sig)))
    head_back = head_back_f.astype(BF16)
    head_back_f = head_back.astype(F32)

    def backward_group(g, acc):
        for i in range(group):
            t = g * group + i
            acc = acc + dot_lanes(
                jnp.where(owner == t, head_back_f, 0.0).astype(BF16), heads[t]
            )
        return acc

    hidden_back = lax.fori_loop(
        0, trainers // group, backward_group, jnp.zeros((elements, depth), F32)
    ).astype(BF16)
    preact_back = (
        hidden_back.astype(F32) * (pre_sig * (1.0 + preact * (1.0 - pre_sig)))
    ).astype(BF16)
    part[...] = dot_rows(node_input, preact_back)
    packed[...] = (
        dot_rows(place, jnp.concatenate([hidden, head_back], axis=0))
        .astype(BF16)
        .reshape(packed.shape)
    )

    out_hi = out_part.astype(BF16).astype(F32)
    out_lo = out_part - out_hi
    sub = lax.broadcasted_iota(jnp.int32, (8, depth), 0)
    out_rows = jnp.where(sub == 0, out_hi, jnp.where(sub == 1, out_lo, 0.0))

    def message(d):
        chunk = part[pl.ds(pl.multiple_of((d % chunks) * 8, 8), 8), :]
        trainer = (d // (n_gz * n_ta)) * n_ta + d % n_ta
        tail = jnp.concatenate([chunk, out_rows], axis=0).astype(BF16)
        return packed[trainer], tail

    def send_message(s, carry):
        d = (me + s) % count
        routed, tail = message(d)
        msg_send[d, 0 : 2 * half, :] = routed
        msg_send[d, 2 * half : 2 * half + 16, :] = tail
        pltpu.make_async_remote_copy(
            src_ref=msg_send.at[d],
            dst_ref=msg_buf.at[me],
            send_sem=msg_ssem,
            recv_sem=msg_rsem,
            device_id=coords(d),
            device_id_type=MESH,
        ).start()
        return carry

    lax.fori_loop(1, count, send_message, 0)
    routed, tail = message(me)
    msg_buf[me, 0 : 2 * half, :] = routed
    msg_buf[me, 2 * half : 2 * half + 16, :] = tail

    def residual_planes(g, carry):
        r_ref[pl.ds(g * EL, EL)] = combine(res, g * EL)
        return carry

    lax.fori_loop(0, cx // EL, residual_planes, 0)

    all_bytes(msg_buf, count - 1, msg_rsem).wait()
    block = 32

    def sum_tails(b, acc):
        start = b * block
        return acc + jnp.sum(
            msg_buf[pl.ds(start, block), 2 * half : 2 * half + 16, :].astype(F32), axis=0
        )

    tails = lax.fori_loop(0, count // block, sum_tails, jnp.zeros((16, depth), F32))

    def send_fin(s, carry):
        pltpu.make_async_remote_copy(
            src_ref=fin.at[me],
            dst_ref=fin.at[me],
            send_sem=fin_ssem,
            recv_sem=fin_rsem,
            device_id=coords((me + s) % count),
            device_id_type=MESH,
        ).start()
        return carry

    if chunks == count:
        fin[me] = tails[0:8]
        lax.fori_loop(1, count, send_fin, 0)
    else:

        @pl.when(me < chunks)
        def own_chunk():
            fin[me] = tails[0:8]
            lax.fori_loop(1, count, send_fin, 0)

    og_ref[...] = tails[8:9] + tails[9:10]

    def sum_heads(b, acc):
        both = msg_buf[pl.ds(b * block, block), 0 : 2 * half, :].astype(F32)
        hid = both[:, 0:half].reshape(block * half, depth).astype(BF16)
        back = both[:, half : 2 * half].reshape(block * half, depth).astype(BF16)
        return acc + dot_rows(hid, back)

    hg_ref[0] = lax.fori_loop(0, count // block, sum_heads, jnp.zeros((depth, depth), F32))

    if chunks == count:
        all_bytes(fin, count - 1, fin_rsem).wait()
        all_bytes(fin, count - 1, fin_ssem).wait()
    else:

        @pl.when(me < chunks)
        def owner_waits():
            all_bytes(fin, chunks - 1, fin_rsem).wait()

            def one_send(s, carry):
                pltpu.make_async_copy(fin.at[me], fin.at[me], fin_ssem).wait()
                return carry

            lax.fori_loop(1, count, one_send, 0)

        @pl.when(me >= chunks)
        def others_wait():
            all_bytes(fin, chunks, fin_rsem).wait()

    ig_ref[...] = fin[...].reshape(ig_ref.shape)
    all_bytes(heads, trainers - 1, heads_send).wait()
    all_bytes(gram_buf, count - 1, gram_ssem).wait()
    all_bytes(msg_buf, count - 1, msg_ssem).wait()


def local(
    sizes,
    right_side,
    diagonal,
    coupling,
    wall_owner,
    neighbours,
    input_weight,
    head_weights,
    output_weight,
):
    n_gx, n_gz, n_ta = sizes
    count, trainers = n_gx * n_gz * n_ta, n_gx * n_ta
    cx, cz, depth = right_side.shape
    ex, ez = cx + 2 * HX, cz + 2 * HZ
    elements = wall_owner.shape[0]
    capacity = max(2, 2 * elements // trainers)
    half = -(-capacity // 8) * 8
    wide = input_weight.shape[0]
    chunks = min(count, wide // 8)
    vmem = pl.BlockSpec(memory_space=pltpu.VMEM)
    hbm = pl.BlockSpec(memory_space=pl.ANY)
    dma = pltpu.SemaphoreType.DMA
    field, residual, input_grad, head_grad, output_grad = pl.pallas_call(
        functools.partial(kernel, sizes),
        out_shape=(
            jax.ShapeDtypeStruct(right_side.shape, F32),
            jax.ShapeDtypeStruct(right_side.shape, F32),
            jax.ShapeDtypeStruct((wide, depth), F32),
            jax.ShapeDtypeStruct((1, depth, depth), F32),
            jax.ShapeDtypeStruct((1, depth), F32),
        ),
        in_specs=[hbm, hbm] + [vmem] * 6,
        out_specs=(vmem,) * 5,
        scratch_shapes=[
            pltpu.VMEM((ITERS + 2, ex, ez, depth), F32),
            pltpu.VMEM((ex, ez, depth), F32),
            pltpu.VMEM((trainers, depth, depth), BF16),
            pltpu.VMEM((2 * depth, 2 * depth), BF16),
            pltpu.VMEM((1, depth), F32),
            pltpu.VMEM((count, 1, depth), F32),
            pltpu.VMEM((elements * EL, depth), F32),
            pltpu.VMEM((trainers, 2 * half, depth), BF16),
            pltpu.VMEM((wide, depth), F32),
            pltpu.VMEM((count, 2 * half + 16, depth), BF16),
            pltpu.VMEM((count, 2 * half + 16, depth), BF16),
            pltpu.VMEM((chunks, 8, depth), F32),
            dma((2,)),
            dma((2, len(DIRS))),
            dma((2, len(DIRS))),
            dma,
            dma,
            dma,
            dma,
            dma,
            dma,
            dma,
            dma,
        ],
        compiler_params=pltpu.CompilerParams(
            collective_id=0, has_side_effects=True, vmem_limit_bytes=44 * 1024 * 1024
        ),
    )(
        right_side,
        diagonal,
        coupling,
        wall_owner,
        neighbours,
        input_weight,
        head_weights,
        output_weight.reshape(1, -1),
    )
    return (field, residual, input_grad, head_grad, output_grad.reshape(-1))


def solution(mesh):
    placed = (
        P(("gx", "ta"), "gz", None),
        P(("gx", "ta"), "gz", None),
        P(),
        P(("gx", "gz", "ta"), None),
        P(("gx", "gz", "ta"), None),
        P(),
        P(("gx", "ta"), None, None),
        P(),
    )
    sizes = tuple(mesh.shape[name] for name in ("gx", "gz", "ta"))
    return jax.shard_map(
        functools.partial(local, sizes),
        mesh=mesh,
        in_specs=placed,
        out_specs=(
            P(("gx", "ta"), "gz", None),
            P(("gx", "ta"), "gz", None),
            P(),
            P(("gx", "ta"), None, None),
            P(),
        ),
        check_vma=False,
    )
```

time: 834 us -> 59.3 us (0.07)
  blocking collectives: 579 us -> 0 us
  waiting for transfers between devices: 130 us -> 0 us
  starting transfers between devices: 53.6 us -> 0 us
  Pallas kernels: 0 us -> 49.6 us
  between operations: 14.3 us -> 0.68 us
  loops' own time: 12.5 us -> 0 us
  local copies, waits for them, and re-layouts: 20.2 us -> 8.58 us
  matrix products: 10.8 us -> 0 us
  other arithmetic: 9.36 us -> 0 us
    psum x14 -> x0, blocking collectives: 579 us -> none  [the longest x7 295 us: global_squares(): return lax.psum(jnp.sum(residual * residual), ('gx', 'gz', 'ta'))]
    psum x2 -> x0, waiting for transfers between devices: 105 us -> none  [the longest x1 105 us: local(): lax.psum((input_part, output_part), ('gx', 'gz', 'ta'))]
    pallas_call x0 -> x1, Pallas kernels: none -> 49.6 us  [local(): pl.pallas_call(functools.partial(kernel, sizes), out_shape=(jax.ShapeDtyp...]
    ppermute x24 -> x0, starting transfers between devices: 37.4 us -> none  [the longest x12 35.1 us: padded_2(): lax.ppermute(lax.slice_in_dim(block, 0, width, axis=dim), axis, backward)]
    all_to_all x3 -> x0, starting transfers between devices: 16.1 us -> none  [the longest x1 7.09 us: local(): lax.all_to_all(pack(hidden), ('gx', 'ta'), split_axis=0, concat_axis=0, t...]
    all_to_all x3 -> x0, waiting for transfers between devices: 13.6 us -> none  [the longest x1 7.22 us: local(): lax.all_to_all(pack(hidden), ('gx', 'ta'), split_axis=0, concat_axis=0, t...]
    another operation x1 -> x0, loops' own time: 12.5 us -> none  [local(): lax.fori_loop(0, ITERS, plain_iter, (solution_field, residual, right_side...]
    ppermute x24 -> x0, waiting for transfers between devices: 11.4 us -> none  [the longest x12 10.4 us: padded_2(): lax.ppermute(lax.slice_in_dim(block, block.shape[dim] - width, None, axis...]
  transfers between devices with their start and end apart: 29 -> 0, of which waited for: 15 -> 0; matrix products, arithmetic and copies ran while one was open for 1% -> 0% of each run, Pallas kernels for 0% -> 0%
where the time goes in v1:
time: 59.3 us; the launch traced here: 58.9 us
  Pallas kernels  49.6 us (84%)
  local copies, waits for them, and re-layouts  8.58 us (14%)
  between operations  0.68 us (1%)
    pallas_call x1, Pallas kernels, local(): pl.pallas_call(functools.partial(kernel, sizes), out_shape=(jax.ShapeDtyp...  49.6 us
    unnamed x21, local copies, waits for them, and re-layouts  8.58 us

profile of v1, /device:TPU:0, one launch (start us, length us, event | category | flops | bytes accessed | tf_op | source)
XLA Modules:
  0.0 58.9 jit_solution(18080499299481759419)
XLA Ops:
  0.6 0.0 copy-start.6
  0.6 0.0 copy-start.2
  0.7 0.6 %copy-done.6 = s32[64,1]{0,1:T(1,128)S(1)} copy-done((s32[64,1]{0,1:T(1,128)S(1)}, s32[64,1]{0,1:T(1,128)}, u32[]{:S(2)}) %copy-start.6) | copy-done | bytes 280
  1.3 0.1 copy.13.owner_ref
  1.4 0.0 copy-start.5
  1.4 0.8 %copy.14.neigh_ref = s32[64,4]{1,0:T(8,128)S(1)} copy(s32[64,4]{0,1:T(4,128)} %param.12) | data formatting | bytes 2048 | tf_op args[4]
  2.2 0.0 copy-done.2
  2.2 0.0 copy-done.5
  2.2 0.0 copy-start
  2.2 1.0 %copy-done = f32[32,32,128]{2,1,0:T(8,128)S(1)} copy-done((f32[32,32,128]{2,1,0:T(8,128)S(1)}, f32[32,32,128]{2,1,0:T(8,128)}, u32[]{:S(2)}) %copy-start) | copy-done | bytes 524312
  3.2 0.0 copy-start.1
  3.2 1.0 %copy-done.1 = f32[32,32,128]{2,1,0:T(8,128)S(1)} copy-done((f32[32,32,128]{2,1,0:T(8,128)S(1)}, f32[32,32,128]{2,1,0:T(8,128)}, u32[]{:S(2)}) %copy-start.1) | copy-done | bytes 524312
  4.3 0.0 copy-start.3
  4.3 0.8 %copy-done.3 = bf16[256,128]{1,0:T(8,128)(2,1)S(1)} copy-done((bf16[256,128]{1,0:T(8,128)(2,1)S(1)}, bf16[256,128]{1,0:T(8,128)(2,1)}, u32[]{:S(2)}) %copy-start.3) | copy-done | bytes 65560
  5.1 0.0 copy-start.4
  5.1 0.8 %copy-done.4 = bf16[1,128,128]{2,1,0:T(8,128)(2,1)S(1)} copy-done((bf16[1,128,128]{2,1,0:T(8,128)(2,1)S(1)}, bf16[1,128,128]{2,1,0:T(8,128)(2,1)}, u32[]{:S(2)}) %copy-start.4) | copy-done | bytes 32792
  5.9 49.6 %shard_map.119 = (f32[32,32,128]{2,1,0:T(8,128)S(1)}, f32[32,32,128]{2,1,0:T(8,128)S(1)}, f32[256,128]{1,0:T(8,128)S(1)}, f32[1,128,128]{2,1,0:T(8,128)S(1)}, f32[1,128]{1,0:T(1,128)S(1)}) custom-call(f32[32,32,128]{2,1,0:T(8,128)S(1)} %copy-done, f32[32,32,128]{2,1,0:T(8,128)S(1)} %copy-done.1, f32[128,128]{1,0:T(8,128)S(1)} %copy-done.2, ...), custom_call_target="tpu_custom_call" | custom-call | tf_op jit(solution)/shard_map/pallas_call | solution.py:509
  55.5 0.8 %copy.20 = f32[32,32,128]{2,1,0:T(8,128)} copy(f32[32,32,128]{2,1,0:T(8,128)S(1)} %get-tuple-element.20) | data formatting | bytes 1048576
  56.3 0.8 %copy.21 = f32[32,32,128]{2,1,0:T(8,128)} copy(f32[32,32,128]{2,1,0:T(8,128)S(1)} %get-tuple-element.21) | data formatting | bytes 1048576
  57.1 0.7 %copy.22 = f32[256,128]{1,0:T(8,128)} copy(f32[256,128]{1,0:T(8,128)S(1)} %get-tuple-element.22) | data formatting | bytes 262144
  57.7 0.6 %copy.23 = f32[1,128,128]{2,1,0:T(8,128)} copy(f32[1,128,128]{2,1,0:T(8,128)S(1)} %get-tuple-element.23) | data formatting | bytes 131072
  58.4 0.5 copy.24
Async XLA Ops:
  0.6 0.7 %copy-start.6 = (s32[64,1]{0,1:T(1,128)S(1)}, s32[64,1]{0,1:T(1,128)}, u32[]{:S(2)}) copy-start(s32[64,1]{0,1:T(1,128)} %param.11) | copy-start | bytes 772
  0.6 1.5 %copy-start.2 = (f32[128,128]{1,0:T(8,128)S(1)}, f32[128,128]{1,0:T(8,128)}, u32[]{:S(2)}) copy-start(f32[128,128]{1,0:T(8,128)} %coup_ref.1) | copy-start | bytes 196612
  1.4 0.8 %copy-start.5 = (f32[128]{0:T(128)S(1)}, f32[128]{0:T(128)}, u32[]{:S(2)}) copy-start(f32[128]{0:T(128)} %param.15) | copy-start | bytes 1540
  2.2 1.0 %copy-start = (f32[32,32,128]{2,1,0:T(8,128)S(1)}, f32[32,32,128]{2,1,0:T(8,128)}, u32[]{:S(2)}) copy-start(f32[32,32,128]{2,1,0:T(8,128)} %rhs_hbm.1) | copy-start | bytes 1572868
  3.2 1.0 %copy-start.1 = (f32[32,32,128]{2,1,0:T(8,128)S(1)}, f32[32,32,128]{2,1,0:T(8,128)}, u32[]{:S(2)}) copy-start(f32[32,32,128]{2,1,0:T(8,128)} %diag_hbm.1) | copy-start | bytes 1572868
  4.3 0.8 %copy-start.3 = (bf16[256,128]{1,0:T(8,128)(2,1)S(1)}, bf16[256,128]{1,0:T(8,128)(2,1)}, u32[]{:S(2)}) copy-start(bf16[256,128]{1,0:T(8,128)(2,1)} %w_in_ref.1) | copy-start | bytes 196612
  5.1 0.8 %copy-start.4 = (bf16[1,128,128]{2,1,0:T(8,128)(2,1)S(1)}, bf16[1,128,128]{2,1,0:T(8,128)(2,1)}, u32[]{:S(2)}) copy-start(bf16[1,128,128]{2,1,0:T(8,128)(2,1)} %head_ref.1) | copy-start | bytes 98308

commit v2 on v1

v2 whole, which is shorter than its diff:
```python
import functools
import jax
import jax.numpy as jnp
from jax import lax
from jax.experimental import pallas as pl
from jax.experimental.pallas import tpu as pltpu
from jax.sharding import PartitionSpec as P

EL = 4
ITERS = 6
HX = ITERS
HZ = 8
CENTRE = 5.3
SPREAD = 5.4
PLANES = 14
MESH = pl.DeviceIdType.MESH
F32 = jnp.float32
BF16 = jnp.bfloat16

def tree_sum(terms):
    terms = list(terms)
    while len(terms) > 1:
        terms = [
            terms[i] + terms[i + 1] if i + 1 < len(terms) else terms[i]
            for i in range(0, len(terms), 2)
        ]
    return terms[0]


def sigmoid(v):
    return 1.0 / (1.0 + jnp.exp(-v))


def dot_rows(a, b):
    return lax.dot_general(a, b, (((0,), (0,)), ((), ())), preferred_element_type=F32)


def dot_lanes(a, b):
    return lax.dot_general(a, b, (((1,), (1,)), ((), ())), preferred_element_type=F32)


def kernel(
    sizes,
    rhs_hbm,
    diag_hbm,
    coup_hbm,
    owner_hbm,
    neigh_hbm,
    w_in_hbm,
    head_hbm,
    w_out_hbm,
    x_ref,
    r_ref,
    ig_ref,
    hg_ref,
    og_ref,
    basis,
    diag,
    coup_ref,
    owner_ref,
    neigh_ref,
    w_in_ref,
    head_ref,
    w_out_ref,
    c_split,
    gram_pair,
    gram_buf,
    pooled,
    fwd_send,
    fwd_buf,
    ret_send,
    ret_buf,
    part_send,
    part_buf,
    pair_heads,
    pair_sums,
    fin,
    load_sem,
    halo_send,
    halo_recv,
    corner_send,
    corner_recv,
    group_send,
    group_recv,
):
    n_gx, n_gz, n_ta = sizes
    trainers = n_gx * n_ta
    cx, cz, depth = x_ref.shape
    ex, ez = cx + 2 * HX, cz + 2 * HZ
    elements = owner_ref.shape[1]
    half = fwd_buf.shape[1] // 2
    chunks, chunk = fin.shape[0], fin.shape[1]
    gx, gz, ta = lax.axis_index("gx"), lax.axis_index("gz"), lax.axis_index("ta")
    row = gx * n_ta + ta

    def in_row(there):
        return (there // n_ta, gz, there % n_ta)

    loads = [
        pltpu.make_async_copy(source, target, load_sem.at[i])
        for i, (source, target) in enumerate(
            (
                (rhs_hbm, basis.at[1, pl.ds(HX, cx), pl.ds(HZ, cz), :]),
                (diag_hbm, diag.at[pl.ds(HX, cx), pl.ds(HZ, cz), :]),
                (coup_hbm, coup_ref),
                (owner_hbm, owner_ref),
                (neigh_hbm, neigh_ref),
                (w_in_hbm, w_in_ref),
                (head_hbm, head_ref),
                (w_out_hbm, w_out_ref),
            )
        )
    ]
    for load in loads:
        load.start()

    barrier = pltpu.get_barrier_semaphore()

    def greet(s, carry):
        pl.semaphore_signal(
            barrier, inc=1, device_id=in_row((row + s) % trainers), device_id_type=MESH
        )
        return carry

    lax.fori_loop(1, trainers, greet, 0)
    for s in range(1, n_gz):
        pl.semaphore_signal(
            barrier, inc=1, device_id=(gx, (gz + s) % n_gz, ta), device_id_type=MESH
        )

    basis[0] = jnp.zeros(basis.shape[1:], F32)
    for load in loads:
        load.wait()
    scaled = coup_ref[...] * (2.0 / SPREAD)
    c_hi = scaled.astype(BF16)
    c_lo = (scaled - c_hi.astype(F32)).astype(BF16)
    c_split[0:depth, 0:depth] = c_hi
    c_split[0:depth, depth : 2 * depth] = c_lo
    c_split[depth : 2 * depth, 0:depth] = c_hi
    c_split[depth : 2 * depth, depth : 2 * depth] = c_lo
    pl.semaphore_wait(barrier, trainers - 1 + n_gz - 1)

    def edge_copy(ref, src_x, dst_x, nx, src_z, dst_z, nz, target, sends, recvs, i):
        return pltpu.make_async_remote_copy(
            src_ref=ref.at[pl.ds(src_x, nx), pl.ds(src_z, nz), :],
            dst_ref=ref.at[pl.ds(dst_x, nx), pl.ds(dst_z, nz), :],
            send_sem=sends.at[i],
            recv_sem=recvs.at[i],
            device_id=target,
            device_id_type=MESH,
        )

    fields = (basis.at[1], diag)
    after, before = in_row((row + 1) % trainers), in_row((row + trainers - 1) % trainers)
    higher, lower = (gx, (gz + 1) % n_gz, ta), (gx, (gz + n_gz - 1) % n_gz, ta)
    x_copies, z_copies, corners = [], [], []
    for j, ref in enumerate(fields):
        wide = HX - j
        for up, (target, src, dst) in enumerate(
            ((after, HX + cx - wide, HX - wide), (before, HX, HX + cx))
        ):
            x_copies.append(
                edge_copy(
                    ref, src, dst, wide, HZ, HZ, cz, target, halo_send, halo_recv, 2 * j + up
                )
            )
    for j, ref in enumerate(fields):
        for up, (target, src, dst) in enumerate(((higher, cz, 0), (lower, HZ, HZ + cz))):
            z_copies.append(
                edge_copy(
                    ref, HX, HX, cx, src, dst, HZ, target, halo_send, halo_recv, 4 + 2 * j + up
                )
            )
            for side, x0 in enumerate((1, HX + cx)):
                corners.append(
                    edge_copy(
                        ref, x0, x0, HX - 1, src, dst, HZ, target,
                        corner_send, corner_recv, 4 * j + 2 * up + side,
                    )
                )
    for copy in x_copies + z_copies:
        copy.start()

    owner = owner_ref[...]
    ids = lax.broadcasted_iota(jnp.int32, (128, elements), 0)
    hits = jnp.where(owner == ids, 1.0, 0.0).astype(BF16)
    same = dot_rows(hits, hits)
    e_row = lax.broadcasted_iota(jnp.int32, (elements, elements), 0)
    e_col = lax.broadcasted_iota(jnp.int32, (elements, elements), 1)
    rank = jnp.sum(jnp.where(e_row < e_col, same, 0.0), axis=0, keepdims=True)
    slot = owner.astype(F32) * (2.0 * half) + rank
    slot_ids = lax.broadcasted_iota(jnp.int32, (trainers * 2 * half, elements), 0).astype(F32)
    place_hidden = jnp.where(slot == slot_ids, 1.0, 0.0).astype(BF16)
    place_shear = jnp.where(slot + half == slot_ids, 1.0, 0.0).astype(BF16)
    place = jnp.concatenate([place_hidden, place_shear], axis=1)
    neigh = neigh_ref[...]
    links = jnp.zeros((elements, elements), F32)
    for j in range(neigh.shape[0]):
        links = links + jnp.where(neigh[j : j + 1, :] == e_row, 1.0, 0.0)
    links = links.astype(BF16)
    pool_cols = lax.broadcasted_iota(jnp.int32, (elements, elements * EL), 1)
    pool_rows = lax.broadcasted_iota(jnp.int32, (elements, elements * EL), 0) * EL
    pool_map = jnp.where(
        (pool_cols >= pool_rows) & (pool_cols < pool_rows + EL), 1.0, 0.0
    ).astype(F32)

    for copy in x_copies:
        copy.wait_recv()
    for copy in corners:
        copy.start()
    for copy in z_copies + corners:
        copy.wait_recv()

    rows = PLANES * ez

    def grow(k, carry):
        def planes(j, inner_carry):
            x0 = 1 + PLANES * j
            cur = basis[k + 1, pl.ds(x0, PLANES)].reshape(rows, depth)
            up = basis[k + 1, pl.ds(x0 - 1, PLANES)].reshape(rows, depth)
            down = basis[k + 1, pl.ds(x0 + 1, PLANES)].reshape(rows, depth)
            prev = basis[k, pl.ds(x0, PLANES)].reshape(rows, depth)
            own = diag[pl.ds(x0, PLANES)].reshape(rows, depth)
            hi = cur.astype(BF16)
            lo = (cur - hi.astype(F32)).astype(BF16)
            prod = jnp.dot(
                jnp.concatenate([hi, lo], axis=1), c_split[...], preferred_element_type=F32
            )
            beside = (up + down) + (pltpu.roll(cur, 1, 0) + pltpu.roll(cur, rows - 1, 0))
            horizontal = ((own + (4.0 - CENTRE)) * cur - beside) * (2.0 / SPREAD)
            new = horizontal + (prod[:, 0:depth] + prod[:, depth : 2 * depth]) - prev
            basis[k + 2, pl.ds(x0, PLANES)] = new.reshape(PLANES, ez, depth)
            return inner_carry

        return lax.fori_loop(0, (ex - 2) // PLANES, planes, carry)

    lax.fori_loop(0, ITERS, grow, 0)

    pairs = [(i, j) for i in range(ITERS + 1) for j in range(i, ITERS + 1)]
    spot = {pair: k for k, pair in enumerate(pairs)}

    def gram_plane(x, sums):
        sums = list(sums)
        for z in range(0, cz, 8):
            vecs = [basis[k + 1, HX + x, HZ + z : HZ + z + 8, :] for k in range(ITERS + 1)]
            for q, (i, j) in enumerate(pairs):
                sums[q] = sums[q] + vecs[i] * vecs[j]
        return tuple(sums)

    sums = lax.fori_loop(
        0, cx, gram_plane, tuple(jnp.zeros((8, depth), F32) for unused in pairs)
    )
    lane = lax.broadcasted_iota(jnp.int32, (8, depth), 1)
    mine = jnp.zeros((8, depth), F32)
    for q, value in enumerate(sums):
        mine = mine + jnp.where(lane == q, jnp.sum(value, axis=1, keepdims=True), 0.0)
    mine = jnp.sum(mine, axis=0, keepdims=True)

    def all_bytes(ref, number, sem):
        there = ref.at[pl.ds(0, number)]
        return pltpu.make_async_copy(there, there, sem)

    def to_pair(ref, i):
        for s in range(1, n_gz):
            pltpu.make_async_remote_copy(
                src_ref=ref.at[gz],
                dst_ref=ref.at[gz],
                send_sem=group_send.at[i],
                recv_sem=group_recv.at[i],
                device_id=(gx, (gz + s) % n_gz, ta),
                device_id_type=MESH,
            ).start()

    def to_row(source, ref, i):
        def send(s, carry):
            there = (row + s) % trainers
            pltpu.make_async_remote_copy(
                src_ref=source(there),
                dst_ref=ref.at[row],
                send_sem=group_send.at[i],
                recv_sem=group_recv.at[i],
                device_id=in_row(there),
                device_id_type=MESH,
            ).start()
            return carry

        lax.fori_loop(1, trainers, send, 0)

    gram_pair[gz] = mine
    to_pair(gram_pair, 0)
    all_bytes(gram_pair, n_gz - 1, group_recv.at[0]).wait()
    gram_buf[row] = jnp.sum(gram_pair[...], axis=0)
    to_row(lambda there: gram_buf.at[row], gram_buf, 1)
    all_bytes(gram_buf, trainers - 1, group_recv.at[1]).wait()
    total = jnp.sum(gram_buf[...], axis=0)

    gram = {}
    for (i, j), q in spot.items():
        value = jnp.broadcast_to(total[0:1, q : q + 1], (8, depth))
        gram[i, j] = value
        gram[j, i] = value

    def inner(a, b):
        return tree_sum(
            a[i] * tree_sum(gram[i, j] * b[j] for j in range(len(b))) for i in range(len(a))
        )

    def operate(a):
        out = []
        for i in range(len(a) + 1):
            terms = []
            if i < len(a):
                terms.append(CENTRE * a[i])
            if i >= 1:
                terms.append((SPREAD / 2) * a[i - 1])
            if i + 1 < len(a):
                terms.append((SPREAD / 2) * a[i + 1])
            out.append(tree_sum(terms))
        return out

    one = jnp.ones((8, depth), F32)
    res, way, sol = [one], [one], []
    norm_now = gram[0, 0]
    for it in range(ITERS):
        applied = operate(way)
        step = norm_now / inner(way, applied)
        sol = [
            sol[i] + step * way[i] if i < len(sol) else step * way[i] for i in range(len(way))
        ]
        res = [
            res[i] - step * applied[i] if i < len(res) else -(step * applied[i])
            for i in range(len(applied))
        ]
        if it < ITERS - 1:
            norm_next = inner(res, res)
            ratio = norm_next / norm_now
            way = [res[i] + ratio * way[i] if i < len(way) else res[i] for i in range(len(res))]
            norm_now = norm_next

    def combine(coefs, x0):
        return tree_sum(
            coefs[k][None]
            * basis[k + 1, pl.ds(HX + x0, EL), HZ : HZ + cz, :].reshape(EL * cz // 8, 8, depth)
            for k in range(len(coefs))
        ).reshape(EL, cz, depth)

    def solve_planes(g, carry):
        field = combine(sol, g * EL)
        x_ref[pl.ds(g * EL, EL)] = field
        pooled[pl.ds(pl.multiple_of(g * cz, cz), cz), :] = jnp.sum(field, axis=0)
        return carry

    lax.fori_loop(0, cx // EL, solve_planes, 0)

    feat = (
        jnp.dot(
            pool_map, pooled[...], precision=lax.Precision.HIGHEST, preferred_element_type=F32
        )
        * (1.0 / EL)
    )
    shear = (feat[:, 1:2] - feat[:, 0:1]).astype(BF16)
    wall_feat = feat.astype(BF16)
    graph_mean = (dot_rows(links, wall_feat) * 0.25).astype(BF16)
    node_input = jnp.concatenate([wall_feat, graph_mean], axis=1)
    preact = jnp.dot(node_input, w_in_ref[...], preferred_element_type=F32)
    pre_sig = sigmoid(preact)
    hidden = (preact * pre_sig).astype(BF16)
    shears = jnp.broadcast_to(shear.astype(F32), (elements, depth)).astype(BF16)
    fwd_send[...] = (
        jnp.dot(
            place, jnp.concatenate([hidden, shears], axis=0), preferred_element_type=F32
        )
        .astype(BF16)
        .reshape(fwd_send.shape)
    )
    to_row(lambda there: fwd_send.at[there], fwd_buf, 2)
    fwd_buf[row] = fwd_send[row]

    def residual_planes(g, carry):
        r_ref[pl.ds(g * EL, EL)] = combine(res, g * EL)
        return carry

    lax.fori_loop(0, cx // EL, residual_planes, 0)

    all_bytes(fwd_buf, trainers - 1, group_recv.at[2]).wait()
    arrived = fwd_buf[...].astype(F32)
    slots = trainers * half
    hid = arrived[:, 0:half].reshape(slots, depth).astype(BF16)
    own_shear = arrived[:, half : 2 * half].reshape(slots, depth)[:, 0:1]
    own_head = head_ref[0]
    head_pre = jnp.dot(hid, own_head, preferred_element_type=F32)
    head_sig = sigmoid(head_pre)
    head_out = head_pre * head_sig
    w_out = w_out_ref[...]
    predicted = jnp.sum(head_out * w_out, axis=1, keepdims=True)
    misfit = (predicted - own_shear) * (1.0 / elements)
    out_part = jnp.sum(misfit * head_out, axis=0, keepdims=True)
    head_back = (
        misfit * w_out * (head_sig * (1.0 + head_pre * (1.0 - head_sig)))
    ).astype(BF16)
    back = dot_lanes(head_back, own_head).reshape(trainers, half, depth)
    out_hi = out_part.astype(BF16).astype(F32)
    out_lo = out_part - out_hi
    sub = lax.broadcasted_iota(jnp.int32, (half, depth), 0)
    out_rows = jnp.where(sub == 0, out_hi, jnp.where(sub == 1, out_lo, 0.0))
    ret_send[...] = jnp.concatenate(
        [back, jnp.broadcast_to(out_rows[None], (trainers, half, depth))], axis=1
    ).astype(BF16)
    to_row(lambda there: ret_send.at[there], ret_buf, 3)
    ret_buf[row] = ret_send[row]
    pair_heads[gz] = dot_rows(hid, head_back)
    to_pair(pair_heads, 4)
    slope = pre_sig * (1.0 + preact * (1.0 - pre_sig))

    all_bytes(ret_buf, trainers - 1, group_recv.at[3]).wait()
    returned = ret_buf[...]
    hidden_back = dot_rows(place_hidden, returned.reshape(trainers * 2 * half, depth))
    preact_back = (hidden_back * slope).astype(BF16)
    part = dot_rows(node_input, preact_back).astype(BF16)
    part_send[...] = part.reshape(part_send.shape)
    to_row(lambda there: part_send.at[there % chunks], part_buf, 5)
    part_buf[row] = part_send[row % chunks]
    out_plane = jnp.sum(returned[:, half : 2 * half].astype(F32), axis=0)

    all_bytes(part_buf, trainers - 1, group_recv.at[5]).wait()
    pair_sums[gz] = jnp.concatenate(
        [jnp.sum(part_buf[...].astype(F32), axis=0), out_plane], axis=0
    )
    to_pair(pair_sums, 6)
    all_bytes(pair_sums, n_gz - 1, group_recv.at[6]).wait()
    sums = jnp.sum(pair_sums[...], axis=0)

    if chunks == trainers:
        fin[row] = sums[0:chunk].astype(BF16)
        to_row(lambda there: fin.at[row], fin, 7)
    else:

        @pl.when(row < chunks)
        def own_chunk():
            fin[row] = sums[0:chunk].astype(BF16)
            to_row(lambda there: fin.at[row], fin, 7)

    og_ref[...] = sums[chunk : chunk + 1] + sums[chunk + 1 : chunk + 2]
    all_bytes(pair_heads, n_gz - 1, group_recv.at[4]).wait()
    hg_ref[0] = jnp.sum(pair_heads[...], axis=0)

    for copy in x_copies + z_copies + corners:
        copy.wait_send()
    for ref, number, i in (
        (gram_pair, n_gz, 0),
        (gram_buf, trainers, 1),
        (fwd_buf, trainers, 2),
        (ret_buf, trainers, 3),
        (pair_heads, n_gz, 4),
        (part_buf, trainers, 5),
        (pair_sums, n_gz, 6),
    ):
        all_bytes(ref, number - 1, group_send.at[i]).wait()

    if chunks == trainers:
        all_bytes(fin, trainers - 1, group_recv.at[7]).wait()
        all_bytes(fin, trainers - 1, group_send.at[7]).wait()
    else:

        @pl.when(row < chunks)
        def owner_waits():
            all_bytes(fin, chunks - 1, group_recv.at[7]).wait()

            def one_send(s, carry):
                pltpu.make_async_copy(fin.at[row], fin.at[row], group_send.at[7]).wait()
                return carry

            lax.fori_loop(1, trainers, one_send, 0)

        @pl.when(row >= chunks)
        def others_wait():
            all_bytes(fin, chunks, group_recv.at[7]).wait()

    ig_ref[...] = fin[...].astype(F32).reshape(ig_ref.shape)


def hand_over(*refs):
    count = len(refs) // 2
    sems = refs[-1]
    copies = [
        pltpu.make_async_copy(refs[i], refs[count + i], sems.at[i]) for i in range(count)
    ]
    for copy in copies:
        copy.start()
    for copy in copies:
        copy.wait()


def local(
    sizes,
    right_side,
    diagonal,
    coupling,
    wall_owner,
    neighbours,
    input_weight,
    head_weights,
    output_weight,
):
    n_gx, n_gz, n_ta = sizes
    trainers = n_gx * n_ta
    cx, cz, depth = right_side.shape
    ex, ez = cx + 2 * HX, cz + 2 * HZ
    elements = wall_owner.shape[0]
    capacity = max(2, 2 * elements // trainers)
    half = -(-capacity // 8) * 8
    wide = input_weight.shape[0]
    chunks = min(trainers, wide // 16)
    chunk = wide // chunks
    vmem = pl.BlockSpec(memory_space=pltpu.VMEM)
    hbm = pl.BlockSpec(memory_space=pl.ANY)
    dma = pltpu.SemaphoreType.DMA
    rows = (trainers, 2 * half, depth)
    shapes = (
        jax.ShapeDtypeStruct(right_side.shape, F32),
        jax.ShapeDtypeStruct(right_side.shape, F32),
        jax.ShapeDtypeStruct((wide, depth), F32),
        jax.ShapeDtypeStruct((1, depth, depth), F32),
        jax.ShapeDtypeStruct((1, depth), F32),
    )
    results = pl.pallas_call(
        functools.partial(kernel, sizes),
        out_shape=shapes,
        in_specs=[hbm] * 8,
        out_specs=(vmem,) * 5,
        scratch_shapes=[
            pltpu.VMEM((ITERS + 2, ex, ez, depth), F32),
            pltpu.VMEM((ex, ez, depth), F32),
            pltpu.VMEM((depth, depth), F32),
            pltpu.VMEM((1, elements), jnp.int32),
            pltpu.VMEM((neighbours.shape[1], elements), jnp.int32),
            pltpu.VMEM((wide, depth), BF16),
            pltpu.VMEM((1, depth, depth), BF16),
            pltpu.VMEM((1, depth), F32),
            pltpu.VMEM((2 * depth, 2 * depth), BF16),
            pltpu.VMEM((n_gz, 1, depth), F32),
            pltpu.VMEM((trainers, 1, depth), F32),
            pltpu.VMEM((elements * EL, depth), F32),
            pltpu.VMEM(rows, BF16),
            pltpu.VMEM(rows, BF16),
            pltpu.VMEM(rows, BF16),
            pltpu.VMEM(rows, BF16),
            pltpu.VMEM((chunks, chunk, depth), BF16),
            pltpu.VMEM((trainers, chunk, depth), BF16),
            pltpu.VMEM((n_gz, depth, depth), F32),
            pltpu.VMEM((n_gz, chunk + half, depth), F32),
            pltpu.VMEM((chunks, chunk, depth), BF16),
            dma((8,)),
            dma((8,)),
            dma((8,)),
            dma((8,)),
            dma((8,)),
            dma((8,)),
            dma((8,)),
        ],
        compiler_params=pltpu.CompilerParams(
            collective_id=0, has_side_effects=True, vmem_limit_bytes=56 * 1024 * 1024
        ),
    )(
        right_side,
        diagonal,
        coupling,
        wall_owner.reshape(1, -1),
        neighbours.T,
        input_weight,
        head_weights,
        output_weight.reshape(1, -1),
    )
    field, residual, input_grad, head_grad, output_grad = pl.pallas_call(
        hand_over,
        out_shape=shapes,
        in_specs=[hbm] * 5,
        out_specs=(hbm,) * 5,
        scratch_shapes=[dma((5,))],
    )(*results)
    return (field, residual, input_grad, head_grad, output_grad.reshape(-1))


def solution(mesh):
    placed = (
        P(("gx", "ta"), "gz", None),
        P(("gx", "ta"), "gz", None),
        P(),
        P(("gx", "gz", "ta"), None),
        P(("gx", "gz", "ta"), None),
        P(),
        P(("gx", "ta"), None, None),
        P(),
    )
    sizes = tuple(mesh.shape[name] for name in ("gx", "gz", "ta"))
    return jax.shard_map(
        functools.partial(local, sizes),
        mesh=mesh,
        in_specs=placed,
        out_specs=(
            P(("gx", "ta"), "gz", None),
            P(("gx", "ta"), "gz", None),
            P(),
            P(("gx", "ta"), None, None),
            P(),
        ),
        check_vma=False,
    )
```

time: 59.3 us -> 92.5 us (1.56)
  Pallas kernels: 49.6 us -> 91.7 us
  local copies, waits for them, and re-layouts: 8.58 us -> 0 us
    pallas_call x1 -> x2, Pallas kernels: 49.6 us -> 91.7 us  [the longest x1 52.8 us: local(): pl.pallas_call(functools.partial(kernel, sizes), out_shape=shapes, in_spe...]
    unnamed x21 -> x0, local copies, waits for them, and re-layouts: 8.58 us -> none
where the time goes in v2:
time: 92.5 us; the launch traced here: 92.4 us
  Pallas kernels  91.7 us (99%)
    pallas_call x1, Pallas kernels, local(): pl.pallas_call(functools.partial(kernel, sizes), out_shape=shapes, in_spe...  52.8 us
    pallas_call x1, Pallas kernels, local(): pl.pallas_call(hand_over, out_shape=shapes, in_specs=[hbm] * 5, out_specs...  38.9 us

profile of v2, /device:TPU:0, one launch (start us, length us, event | category | flops | bytes accessed | tf_op | source)
XLA Modules:
  0.0 92.4 jit_solution(3599636501803416669)
XLA Ops:
  0.6 52.8 %shard_map.119 = (f32[32,32,128]{2,1,0:T(8,128)}, f32[32,32,128]{2,1,0:T(8,128)}, f32[256,128]{1,0:T(8,128)}, f32[1,128,128]{2,1,0:T(8,128)}, f32[1,128]{1,0:T(1,128)}) custom-call(f32[32,32,128]{2,1,0:T(8,128)} %rhs_hbm.1, f32[32,32,128]{2,1,0:T(8,128)} %diag_hbm.1, f32[128,128]{1,0:T(8,128)} %coup_hbm.1, s32[1,64]{1,0:T(1,128)} %bitcast.5, ...), custom_call_target="tpu_custom_call" | custom-call | tf_op jit(solution)/shard_map/pallas_call | solution.py:526
  53.5 38.9 %shard_map.120 = (f32[32,32,128]{2,1,0:T(8,128)}, f32[32,32,128]{2,1,0:T(8,128)}, f32[256,128]{1,0:T(8,128)}, f32[1,128,128]{2,1,0:T(8,128)}, f32[1,128]{1,0:T(1,128)}) custom-call(f32[32,32,128]{2,1,0:T(8,128)} %get-tuple-element.15.refs_0_, f32[32,32,128]{2,1,0:T(8,128)} %get-tuple-element.16.refs_1_, f32[256,128]{1,0:T(8,128)} %get-tuple-element.17.refs_2_, ...), custom_call_target="tpu_custom_call" | custom-call | tf_op jit(solution)/shard_map/pallas_call | solution.py:574

commit v3 on v2

--- a/solution.py
+++ b/solution.py
@@ -480,15 +480,20 @@
 
 
 def hand_over(*refs):
-    count = len(refs) // 2
-    sems = refs[-1]
-    copies = [
-        pltpu.make_async_copy(refs[i], refs[count + i], sems.at[i]) for i in range(count)
-    ]
-    for copy in copies:
-        copy.start()
-    for copy in copies:
-        copy.wait()
+    count = (len(refs) - 2) // 3
+    load_sem, store_sem = refs[-2:]
+    loads, stores = [], []
+    for i in range(count):
+        source, target, held = refs[i], refs[count + i], refs[2 * count + i]
+        loads.append(pltpu.make_async_copy(source, held, load_sem.at[i]))
+        stores.append(pltpu.make_async_copy(held, target, store_sem.at[i]))
+    for load in loads:
+        load.start()
+    for load, store in zip(loads, stores):
+        load.wait()
+        store.start()
+    for store in stores:
+        store.wait()
 
 
 def local(
@@ -576,7 +581,7 @@
         out_shape=shapes,
         in_specs=[hbm] * 5,
         out_specs=(hbm,) * 5,
-        scratch_shapes=[dma((5,))],
+        scratch_shapes=[pltpu.VMEM(s.shape, s.dtype) for s in shapes] + [dma((5,)), dma((5,))],
     )(*results)
     return (field, residual, input_grad, head_grad, output_grad.reshape(-1))
 

time: 92.5 us -> 55.8 us (0.60)
  Pallas kernels: 91.7 us -> 55 us
    pallas_call x1, Pallas kernels: 38.9 us -> 2.15 us  [local(): pl.pallas_call(hand_over, out_shape=shapes, in_specs=[hbm] * 5, out_specs...]
where the time goes in v3:
time: 55.8 us; the launch traced here: 55.6 us
  Pallas kernels  55 us (99%)
  between operations  0.64 us (1%)
    pallas_call x1, Pallas kernels, local(): pl.pallas_call(functools.partial(kernel, sizes), out_shape=shapes, in_spe...  52.8 us
    pallas_call x1, Pallas kernels, local(): pl.pallas_call(hand_over, out_shape=shapes, in_specs=[hbm] * 5, out_specs...  2.15 us

profile of v3, /device:TPU:0, one launch (start us, length us, event | category | flops | bytes accessed | tf_op | source)
XLA Modules:
  0.0 55.6 jit_solution(13909308183244674382)
XLA Ops:
  0.6 52.8 %shard_map.119 = (f32[32,32,128]{2,1,0:T(8,128)}, f32[32,32,128]{2,1,0:T(8,128)}, f32[256,128]{1,0:T(8,128)}, f32[1,128,128]{2,1,0:T(8,128)}, f32[1,128]{1,0:T(1,128)}) custom-call(f32[32,32,128]{2,1,0:T(8,128)} %rhs_hbm.1, f32[32,32,128]{2,1,0:T(8,128)} %diag_hbm.1, f32[128,128]{1,0:T(8,128)} %coup_hbm.1, s32[1,64]{1,0:T(1,128)} %bitcast.5, ...), custom_call_target="tpu_custom_call" | custom-call | tf_op jit(solution)/shard_map/pallas_call | solution.py:531
  53.5 2.1 %shard_map.120 = (f32[32,32,128]{2,1,0:T(8,128)}, f32[32,32,128]{2,1,0:T(8,128)}, f32[256,128]{1,0:T(8,128)}, f32[1,128,128]{2,1,0:T(8,128)}, f32[1,128]{1,0:T(1,128)}) custom-call(f32[32,32,128]{2,1,0:T(8,128)} %get-tuple-element.15.refs_0_, f32[32,32,128]{2,1,0:T(8,128)} %get-tuple-element.16.refs_1_, f32[256,128]{1,0:T(8,128)} %get-tuple-element.17.refs_2_, ...), custom_call_target="tpu_custom_call" | custom-call | tf_op jit(solution)/shard_map/pallas_call | solution.py:579
